TPU v7x, 512 devices: a whole 4x4x16 slice. The times are simulated.
512 devices in a mesh: grp: 8 (over x, y_hi), lon: 16 (over z), lat: 4 (over y_lo, core).
Axes of the slice: x: 4, y: 4 (y_hi: 2, y_lo: 2; y = y_hi * 2 + y_lo), z: 16, core: 2. Of those that a mesh axis runs over, the one named last changes fastest.
Arguments:
- tracers: float32 [64, 256, 64, 128], P('grp', 'lon', 'lat'), may hold values from -6 to 6
- fluxes: float32 [2, 3, 256, 64, 128], P(None, None, 'lon', 'lat', 'grp'), may hold values from -0.3 to 0.3
- limiter_mask: int32 [2, 256, 64, 128], P(None, 'lon', 'lat'), may hold values 0 or 1
- diffusion_inverse: float32 [2, 64, 128, 128], P(None, 'lat'), may hold values from 0 to 1, as said below
Outputs:
- transported: float32 [64, 256, 64, 128], P('grp', 'lon', 'lat')
Inputs may be any that keep to these rules, and one draw needn't show every extreme that they name: diffusion_inverse[s, j] is symmetric with positive entries and is the inverse of a symmetric tridiagonal matrix.
All inputs are finite; a program needn't handle non-finite values. No bound on the sum of `limiter_mask` on one device may be relied on, other than what follows from the above.
Results may differ from a plain program's by a relative error of at most 0.0001.
Values sent between devices are 32-bit elements; how exact they have to be, the bound alone decides.
A program may use at most 64 MiB of HBM per device.

v0:
```python
import jax
import jax.numpy as jnp
from jax import lax
from jax.sharding import PartitionSpec as P


def padded_2(x, sides, width, wrap):
    for axis, dim in sides:
        count, length = (lax.axis_size(axis), x.shape[dim])
        up = [(i, (i + 1) % count) for i in range(count if wrap else count - 1)]
        down = [(j, i) for i, j in up]
        last = lax.slice_in_dim(x, length - width, length, axis=dim)
        leading = lax.slice_in_dim(x, 0, width, axis=dim)
        before = lax.ppermute(last, axis, up)
        after = lax.ppermute(leading, axis, down)
        x = jnp.concatenate([before, x, after], axis=dim)
    return x


def third_order(minus_two, minus_one, plus_zero, plus_one, courant):
    return (
        courant * (7.0 * (plus_zero + minus_one) - (plus_one + minus_two)) / 12.0
        + jnp.abs(courant) * (plus_one - minus_two - 3.0 * (plus_zero - minus_one)) / 12.0
    )


def first_order(minus_one, plus_zero, courant):
    return (
        courant * (plus_zero + minus_one) / 2.0 - jnp.abs(courant) * (plus_zero - minus_one) / 2.0
    )


def vertical_change(values, courant, limiter):
    depth = values.shape[-1]
    padded = jnp.pad(values, [(0, 0)] * (values.ndim - 1) + [(2, 2)])
    high = third_order(
        padded[..., 0:depth],
        padded[..., 1 : depth + 1],
        padded[..., 2 : depth + 2],
        padded[..., 3 : depth + 3],
        courant,
    )
    low = first_order(padded[..., 1 : depth + 1], padded[..., 2 : depth + 2], courant)
    level_idx = jnp.arange(depth)
    faces = jnp.where(
        level_idx == 0,
        0.0,
        jnp.where((level_idx == 1) | (level_idx == depth - 1) | (limiter == 1), low, high),
    )
    following = jnp.concatenate([faces[..., 1:], jnp.zeros_like(faces[..., :1])], axis=-1)
    return faces - following


def advect(current, step_flux, limiter, first_row, lat_total):
    per_group, lon_cells, lat_cells, levels_all = current.shape
    joined = jnp.concatenate([current, step_flux[0:2]], axis=0)
    lon_ext = padded_2(joined, (("lon", 1),), 2, True)
    lat_ext = padded_2(joined, (("lat", 2),), 2, False)
    eastward = lon_ext[per_group, 2 : lon_cells + 3]
    northward = lat_ext[per_group + 1, :, 2 : lat_cells + 3]
    lon_vals = lon_ext[:per_group]
    lon_faces = third_order(
        lon_vals[:, 0 : lon_cells + 1],
        lon_vals[:, 1 : lon_cells + 2],
        lon_vals[:, 2 : lon_cells + 3],
        lon_vals[:, 3 : lon_cells + 4],
        eastward,
    )
    change_lon = lon_faces[:, :-1] - lon_faces[:, 1:]
    lat_vals = lat_ext[:per_group]
    high = third_order(
        lat_vals[:, :, 0 : lat_cells + 1],
        lat_vals[:, :, 1 : lat_cells + 2],
        lat_vals[:, :, 2 : lat_cells + 3],
        lat_vals[:, :, 3 : lat_cells + 4],
        northward,
    )
    low = first_order(
        lat_vals[:, :, 1 : lat_cells + 2], lat_vals[:, :, 2 : lat_cells + 3], northward
    )
    face_row = (first_row + jnp.arange(lat_cells + 1))[None, None, :, None]
    lat_faces = jnp.where(
        (face_row == 0) | (face_row == lat_total),
        0.0,
        jnp.where((face_row == 1) | (face_row == lat_total - 1), low, high),
    )
    change_lat = lat_faces[:, :, :-1] - lat_faces[:, :, 1:]
    return current + change_lon + change_lat + vertical_change(current, step_flux[2], limiter)


def diffuse(current, inverse_rows):
    return jnp.einsum("jzk,tijk->tijz", inverse_rows, current, precision=lax.Precision.HIGHEST)


def on_device(tracers, fluxes, limiter_mask, diffusion_inverse):
    lat_cells = tracers.shape[2]
    step_count = fluxes.shape[0]
    lat_total = lax.axis_size("lat") * lat_cells
    first_row = lax.axis_index("lat") * lat_cells
    gathered = lax.all_gather(fluxes, "grp", axis=4, tiled=True)
    current = tracers
    for step_no in range(step_count):
        step_flux = gathered[step_no]
        current = advect(current, step_flux, limiter_mask[step_no], first_row, lat_total)
        current = diffuse(current, diffusion_inverse[step_no])
    return current


def solution(mesh):
    in_specs = (
        P("grp", "lon", "lat", None),
        P(None, None, "lon", "lat", "grp"),
        P(None, "lon", "lat", None),
        P(None, "lat", None, None),
    )
    out_specs = P("grp", "lon", "lat", None)
    return jax.shard_map(
        on_device, mesh=mesh, in_specs=in_specs, out_specs=out_specs, check_vma=False
    )
```

profile of v0, /device:TPU:1, one launch (start us, length us, event | category | flops | bytes accessed | tf_op | source)
XLA Modules:
  0.0 199.7 jit_solution(12924976073795645773)
XLA Ops:
  0.0 1.8 copy.14
  1.9 0.3 copy.17
  2.2 125.8 %all_gather.3 = f32[2,3,16,16,128]{3,2,1,0,4:T(8,128)S(1)} all-gather(f32[2,3,16,16,16]{3,2,1,0,4:T(8,128)S(1)} %copy.14), channel_id=1, replica_groups=mesh['grp'=8,'lon'=16,'lat'=4] {'grp'}, dimensions={4}, use_global_device_ids=true | all-gather | bytes 884736 | tf_op jit(solution)/shard_map/all_gather | solution.py:100
  128.0 2.9 %fusion.35 = (f32[1,2,16,16,128]{3,2,1,0,4:T(8,128)}, f32[1,2,16,16,128]{3,2,1,0,4:T(8,128)}) fusion(f32[2,3,16,16,128]{3,2,1,0,4:T(8,128)S(1)} %all_gather.3), kind=kLoop, calls=%fused_computation.82 | loop fusion | bytes 1048576 | tf_op jit(solution)/shard_map/slice | solution.py:56
  130.9 1.2 copy-done
  132.0 2.7 %copy.31 = f32[1,2,16,16,128]{4,2,1,3,0:T(8,128)S(1)} copy(f32[1,2,16,16,128]{3,2,1,0,4:T(8,128)} %get-tuple-element.17) | data formatting | bytes 524288
  134.8 0.8 pad_maximum_fusion.13
  135.6 12.5 %collective-permute-start = (f32[10,2,16,128]{3,1,0,2:T(2,128)}, f32[10,2,16,128]{3,1,0,2:T(2,128)S(1)}, u32[]{:S(2)}, u32[]{:S(2)}) collective-permute-start(f32[10,2,16,128]{3,1,0,2:T(2,128)} %get-tuple-element.29), channel_id=1, source_target_pairs={{4,0},{8,4},{12,8},{16,12},{20,16},{24,20},{28,24},{32,28},{36,32}... | collective-permute-start | bytes 491528 | tf_op jit(solution)/shard_map/ppermute | solution.py:15
  148.1 1.9 collective-permute-start.1
  150.0 0.8 pad_maximum_fusion.11
  150.8 2.7 %collective-permute-start.2 = (f32[10,16,2,128]{3,1,0,2:T(8,128)}, f32[10,16,2,128]{3,1,0,2:T(8,128)S(1)}, u32[]{:S(2)}, u32[]{:S(2)}) collective-permute-start(f32[10,16,2,128]{3,1,0,2:T(8,128)} %get-tuple-element.33), channel_id=1, source_target_pairs={{1,0},{2,1},{3,2},{5,4},{6,5},{7,6},{9,8},{10,9},{11,10},{13,12},{... | collective-permute-start | bytes 491528 | tf_op jit(solution)/shard_map/ppermute | solution.py:15
  153.5 3.0 %collective-permute-start.3 = (f32[10,16,2,128]{3,1,0,2:T(8,128)}, f32[10,16,2,128]{3,1,0,2:T(8,128)S(1)}, u32[]{:S(2)}, u32[]{:S(2)}) collective-permute-start(f32[10,16,2,128]{3,1,0,2:T(8,128)} %get-tuple-element.34), channel_id=1, source_target_pairs={{0,1},{1,2},{2,3},{4,5},{5,6},{6,7},{8,9},{9,10},{10,11},{12,13},{... | collective-permute-start | bytes 491528 | tf_op jit(solution)/shard_map/ppermute | solution.py:14
  156.5 2.8 %slice_bitcast_fusion = (f32[16,16,128]{1,0,2:T(8,128)}, f32[16,16,128]{1,0,2:T(8,128)S(1)}) fusion(f32[2,3,16,16,128]{3,2,1,0,4:T(8,128)} %copy-done), kind=kLoop, calls=%fused_computation.22 | loop fusion | bytes 524288 | tf_op jit(solution)/shard_map/mul | solution.py:29
  159.3 3.1 %fusion.33 = (f32[16,16,128]{1,0,2:T(8,128)}, f32[16,16,128]{1,0,2:T(8,128)}) fusion(f32[2,3,16,16,128]{3,2,1,0,4:T(8,128)} %copy-done), kind=kLoop, calls=%fused_computation.80 | loop fusion | flops 65536 | bytes 524288 | tf_op jit(solution)/shard_map/abs | solution.py:29
  162.5 0.4 copy.19
  162.9 1.6 copy.22
  164.6 0.9 fusion.19
  165.5 0.6 copy.25
  166.1 1.6 copy.26
  167.8 1.6 copy.27
  169.4 2.7 %copy.32 = f32[1,2,16,16,128]{4,2,1,3,0:T(8,128)S(1)} copy(f32[1,2,16,16,128]{3,2,1,0,4:T(8,128)} %get-tuple-element.18) | data formatting | bytes 524288
  172.1 0.3 slice.288
  172.5 0.0 collective-permute-done
  172.5 0.3 pad_maximum_fusion
  172.9 0.8 add_multiply_fusion.1
  173.7 0.0 collective-permute-done.2
  173.8 0.0 collective-permute-done.3
  173.8 0.3 pad_maximum_fusion.2
  174.1 0.0 copy-start.2
  174.1 0.0 copy-start.3
  174.1 0.7 fusion.1
  174.9 0.5 copy-done.2
  175.3 0.7 copy-done.3
  176.0 2.8 %convolution_bitcast_fusion.1 = f32[8,16,16,128]{3,1,0,2:T(8,128)S(1)} fusion(f32[8,16,17,128]{3,1,0,2:T(8,128)S(1)} %fusion.1, f32[8,17,16,128]{3,1,0,2:T(8,128)S(1)} %add_multiply_fusion.1, f32[2,16,128,128]{3,2,1,0:T(8,128)S(1)} %copy-done.3, f32[8,16,16,128]{3,1,0,2:T(8,128)S(1)} %fusion.19, f32[8,16,16,127]{3,1,0,2:T(8,128)S(1)} %slice.288, ...), kind=kOutput, calls=%fused_computation.17 | convolution fusion | flops 404226048 | bytes 9437184 | tf_op jit(solution)/shard_map/jzk,tijk->tijz/dot_general | solution.py:92
  178.8 0.1 pad_maximum_fusion.9
  179.0 4.6 %collective-permute-start.4 = (f32[10,2,16,128]{3,1,0,2:T(2,128)S(1)}, f32[10,2,16,128]{3,1,0,2:T(2,128)S(1)}, u32[]{:S(2)}, u32[]{:S(2)}) collective-permute-start(f32[10,2,16,128]{3,1,0,2:T(2,128)S(1)} %get-tuple-element.21), channel_id=1, source_target_pairs={{4,0},{8,4},{12,8},{16,12},{20,16},{24,20},{28,24},{32,28},{36,32}... | collective-permute-start | bytes 491528 | tf_op jit(solution)/shard_map/ppermute | solution.py:15
  183.6 1.9 collective-permute-start.5
  185.5 2.1 %collective-permute-start.6 = (f32[10,16,2,128]{3,1,0,2:T(8,128)S(1)}, f32[10,16,2,128]{3,1,0,2:T(8,128)S(1)}, u32[]{:S(2)}, u32[]{:S(2)}) collective-permute-start(f32[10,16,2,128]{3,1,0,2:T(8,128)S(1)} %get-tuple-element.25), channel_id=1, source_target_pairs={{1,0},{2,1},{3,2},{5,4},{6,5},{7,6},{9,8},{10,9},{11,10},{13,12},{... | collective-permute-start | bytes 491528 | tf_op jit(solution)/shard_map/ppermute | solution.py:15
  187.6 3.7 %collective-permute-start.7 = (f32[10,16,2,128]{3,1,0,2:T(8,128)S(1)}, f32[10,16,2,128]{3,1,0,2:T(8,128)S(1)}, u32[]{:S(2)}, u32[]{:S(2)}) collective-permute-start(f32[10,16,2,128]{3,1,0,2:T(8,128)S(1)} %get-tuple-element.26), channel_id=1, source_target_pairs={{0,1},{1,2},{2,3},{4,5},{5,6},{6,7},{8,9},{9,10},{10,11},{12,13},{... | collective-permute-start | bytes 491528 | tf_op jit(solution)/shard_map/ppermute | solution.py:14
  191.3 0.9 fusion.18
  192.2 0.3 slice.303
  192.6 0.7 collective-permute-done.7
  193.3 0.3 pad_maximum_fusion.3
  193.6 0.8 fusion
  194.5 0.3 pad_maximum_fusion.1
  194.8 0.8 add_multiply_fusion
  195.6 2.5 %convolution_bitcast_fusion = f32[8,16,16,128]{3,1,0,2:T(8,128)S(1)} fusion(f32[8,16,17,128]{3,1,0,2:T(8,128)S(1)} %fusion, f32[8,16,16,128]{3,1,0,2:T(8,128)S(1)} %convolution_bitcast_fusion.1, f32[8,17,16,128]{3,1,0,2:T(8,128)S(1)} %add_multiply_fusion, f32[2,16,128,128]{3,2,1,0:T(8,128)S(1)} %copy-done.3, f32[8,16,16,128]{3,1,0,2:T(8,128)S(1)} %fusion.18, ...), kind=kOutput, calls=%fused_computation.16 | convolution fusion | flops 404226048 | bytes 9437184 | tf_op jit(solution)/shard_map/jzk,tijk->tijz/dot_general | solution.py:92
  198.1 1.6 copy.28
  (21 shorter events, 0.2 us)
Async XLA Ops:
  0.0 1.8 copy-start.1
  128.0 4.0 %copy-start = (f32[2,3,16,16,128]{3,2,1,0,4:T(8,128)}, f32[2,3,16,16,128]{3,2,1,0,4:T(8,128)S(1)}, u32[]{:S(2)}) copy-start(f32[2,3,16,16,128]{3,2,1,0,4:T(8,128)S(1)} %all_gather.3) | copy-start | bytes 2359300
  135.6 36.9 %collective-permute-start = (f32[10,2,16,128]{3,1,0,2:T(2,128)}, f32[10,2,16,128]{3,1,0,2:T(2,128)S(1)}, u32[]{:S(2)}, u32[]{:S(2)}) collective-permute-start(f32[10,2,16,128]{3,1,0,2:T(2,128)} %get-tuple-element.29), channel_id=1, source_target_pairs={{4,0},{8,4},{12,8},{16,12},{20,16},{24,20},{28,24},{32,28},{36,32}... | collective-permute-start | bytes 491528 | tf_op jit(solution)/shard_map/ppermute | solution.py:15
  148.1 24.5 %collective-permute-start.1 = (f32[10,2,16,128]{3,1,0,2:T(2,128)}, f32[10,2,16,128]{3,1,0,2:T(2,128)S(1)}, u32[]{:S(2)}, u32[]{:S(2)}) collective-permute-start(f32[10,2,16,128]{3,1,0,2:T(2,128)} %get-tuple-element.30), channel_id=1, source_target_pairs={{0,4},{4,8},{8,12},{12,16},{16,20},{20,24},{24,28},{28,32},{32,36}... | collective-permute-start | bytes 491528 | tf_op jit(solution)/shard_map/ppermute | solution.py:14
  150.8 23.0 %collective-permute-start.2 = (f32[10,16,2,128]{3,1,0,2:T(8,128)}, f32[10,16,2,128]{3,1,0,2:T(8,128)S(1)}, u32[]{:S(2)}, u32[]{:S(2)}) collective-permute-start(f32[10,16,2,128]{3,1,0,2:T(8,128)} %get-tuple-element.33), channel_id=1, source_target_pairs={{1,0},{2,1},{3,2},{5,4},{6,5},{7,6},{9,8},{10,9},{11,10},{13,12},{... | collective-permute-start | bytes 491528 | tf_op jit(solution)/shard_map/ppermute | solution.py:15
  153.5 20.3 %collective-permute-start.3 = (f32[10,16,2,128]{3,1,0,2:T(8,128)}, f32[10,16,2,128]{3,1,0,2:T(8,128)S(1)}, u32[]{:S(2)}, u32[]{:S(2)}) collective-permute-start(f32[10,16,2,128]{3,1,0,2:T(8,128)} %get-tuple-element.34), channel_id=1, source_target_pairs={{0,1},{1,2},{2,3},{4,5},{5,6},{6,7},{8,9},{9,10},{10,11},{12,13},{... | collective-permute-start | bytes 491528 | tf_op jit(solution)/shard_map/ppermute | solution.py:14
  159.3 3.1 %copy-start.4 = (s32[2,16,16,128]{3,2,1,0:T(8,128)S(1)}, s32[2,16,16,128]{3,2,1,0:T(8,128)}, u32[]{:S(2)}) copy-start(s32[2,16,16,128]{3,2,1,0:T(8,128)} %param.6) | copy-start | bytes 786436
  174.1 1.2 copy-start.2
  174.1 1.9 copy-start.3
  178.8 12.5 %copy-start.5 = (pred[16,16,128]{2,0,1:T(8,128)(4,1)S(1)}, pred[16,16,128]{2,0,1:T(8,128)(4,1)}, u32[]{:S(2)}) copy-start(pred[16,16,128]{2,0,1:T(8,128)(4,1)} %copy.25) | copy-start | bytes 98308
  179.0 15.4 %collective-permute-start.4 = (f32[10,2,16,128]{3,1,0,2:T(2,128)S(1)}, f32[10,2,16,128]{3,1,0,2:T(2,128)S(1)}, u32[]{:S(2)}, u32[]{:S(2)}) collective-permute-start(f32[10,2,16,128]{3,1,0,2:T(2,128)S(1)} %get-tuple-element.21), channel_id=1, source_target_pairs={{4,0},{8,4},{12,8},{16,12},{20,16},{24,20},{28,24},{32,28},{36,32}... | collective-permute-start | bytes 491528 | tf_op jit(solution)/shard_map/ppermute | solution.py:15
  183.6 10.9 %collective-permute-start.5 = (f32[10,2,16,128]{3,1,0,2:T(2,128)S(1)}, f32[10,2,16,128]{3,1,0,2:T(2,128)S(1)}, u32[]{:S(2)}, u32[]{:S(2)}) collective-permute-start(f32[10,2,16,128]{3,1,0,2:T(2,128)S(1)} %get-tuple-element.22), channel_id=1, source_target_pairs={{0,4},{4,8},{8,12},{12,16},{16,20},{20,24},{24,28},{28,32},{32,36}... | collective-permute-start | bytes 491528 | tf_op jit(solution)/shard_map/ppermute | solution.py:14
  185.5 7.1 %collective-permute-start.6 = (f32[10,16,2,128]{3,1,0,2:T(8,128)S(1)}, f32[10,16,2,128]{3,1,0,2:T(8,128)S(1)}, u32[]{:S(2)}, u32[]{:S(2)}) collective-permute-start(f32[10,16,2,128]{3,1,0,2:T(8,128)S(1)} %get-tuple-element.25), channel_id=1, source_target_pairs={{1,0},{2,1},{3,2},{5,4},{6,5},{7,6},{9,8},{10,9},{11,10},{13,12},{... | collective-permute-start | bytes 491528 | tf_op jit(solution)/shard_map/ppermute | solution.py:15
  187.6 5.7 %collective-permute-start.7 = (f32[10,16,2,128]{3,1,0,2:T(8,128)S(1)}, f32[10,16,2,128]{3,1,0,2:T(8,128)S(1)}, u32[]{:S(2)}, u32[]{:S(2)}) collective-permute-start(f32[10,16,2,128]{3,1,0,2:T(8,128)S(1)} %get-tuple-element.26), channel_id=1, source_target_pairs={{0,1},{1,2},{2,3},{4,5},{5,6},{6,7},{8,9},{9,10},{10,11},{12,13},{... | collective-permute-start | bytes 491528 | tf_op jit(solution)/shard_map/ppermute | solution.py:14
where the time goes:
time: 200 us
  blocking collectives  126 us (63%)
  starting transfers between devices  32.4 us (16%)
  local copies, waits for them, and re-layouts  23.8 us (12%)
  other arithmetic  11.3 us (6%)
  matrix products  5.29 us (3%)
    all_gather x1, blocking collectives, on_device(): gathered = lax.all_gather(fluxes, 'grp', axis=4, tiled=True)  126 us
    ppermute x4, starting transfers between devices, padded_2(): after = lax.ppermute(leading, axis, down)  21.8 us
    ppermute x4, starting transfers between devices, padded_2(): before = lax.ppermute(last, axis, up)  10.6 us
    unnamed x16, local copies, waits for them, and re-layouts  9.96 us
    dot_general x2, matrix products, diffuse(): jnp.einsum('jzk,tijk->tijz', inverse_rows, current, precision=lax.Precisi...  5.29 us
    mul x3, local copies, waits for them, and re-layouts, first_order(): courant * (plus_zero + minus_one) / 2.0  4.84 us
  transfers between devices with their start and end apart: 8, of which 1 were waited for; matrix products, arithmetic and copies ran while one was open for 10% of the time, Pallas kernels for 0%

commit v1 on v0

v1 whole, which is shorter than its diff:
```python
import functools

import jax
import jax.numpy as jnp
from jax import lax
from jax.experimental import pallas as pl
from jax.experimental.pallas import tpu as pltpu
from jax.sharding import PartitionSpec as P

MESH = pl.DeviceIdType.MESH
LANES = 128
POINTS = 13


def faces(courant, first=None):
    plus, minus = jnp.maximum(courant, 0.0), jnp.minimum(courant, 0.0)
    p, m = plus * (1.0 / 6.0), minus * (1.0 / 6.0)
    a, b, c, d = -p, 5.0 * p + 2.0 * m, 2.0 * p + 5.0 * m, -m
    if first is not None:
        a, b = jnp.where(first, 0.0, a), jnp.where(first, plus, b)
        c, d = jnp.where(first, minus, c), jnp.where(first, 0.0, d)
    return a, b, c, d


def spread(low, high):
    a, b, c, d = low
    e, f, g, h = high
    return a, b - e, c - f, d - g, -h


def block_transpose(blocks, lane):
    blocks = list(blocks)
    for bit in (1, 2, 4):
        odd = (lane // (16 * bit)) % 2 == 1
        for g in range(8):
            if g & bit:
                continue
            low, high = blocks[g], blocks[g + bit]
            blocks[g] = jnp.where(odd, pltpu.roll(high, 16 * bit, 1), low)
            blocks[g + bit] = jnp.where(odd, high, pltpu.roll(low, LANES - 16 * bit, 1))
    return blocks


def kernel(
    tracers, fluxes, limiter, inverse, out,
    shard, gath, near, ext, start, field, given, weights, coef, courant, lim, split, done,
    in_sem, out_sem, near_send, near_recv, ext_send, ext_recv, gath_send, gath_recv,
    halo_send, halo_recv, lon_send, lon_recv, lat_send, lat_recv,
):
    groups, lons, lats = lax.axis_size("grp"), lax.axis_size("lon"), lax.axis_size("lat")
    grp, lon, lat = lax.axis_index("grp"), lax.axis_index("lon"), lax.axis_index("lat")
    east, west = lax.rem(lon + 1, lons), lax.rem(lon + lons - 1, lons)
    has_south, has_north = lat > 0, lat < lats - 1
    south, north = lat - 1, lat + 1
    peers = [lax.rem(grp + d, groups) for d in range(1, groups)]
    lane = lax.broadcasted_iota(jnp.int32, (8, LANES), 1)
    sub = lax.broadcasted_iota(jnp.int32, (8, LANES), 0)

    def remote(src, dst, send, recv, where):
        return pltpu.make_async_remote_copy(
            src_ref=src, dst_ref=dst, send_sem=send, recv_sem=recv,
            device_id=where, device_id_type=MESH,
        )

    loads = [
        pltpu.make_async_copy(fluxes.at[0], shard.at[0], in_sem.at[0]),
        pltpu.make_async_copy(tracers, start, in_sem.at[1]),
        pltpu.make_async_copy(fluxes.at[1], shard.at[1], in_sem.at[2]),
        pltpu.make_async_copy(limiter, lim, in_sem.at[3]),
        pltpu.make_async_copy(inverse, given, in_sem.at[4]),
    ]
    for load in loads:
        load.start()

    barrier = pltpu.get_barrier_semaphore()
    for peer in peers:
        pl.semaphore_signal(barrier, inc=1, device_id={"grp": peer}, device_id_type=MESH)
    for side in (east, west):
        pl.semaphore_signal(barrier, inc=1, device_id={"lon": side}, device_id_type=MESH)

    @pl.when(has_south)
    def _():
        pl.semaphore_signal(barrier, inc=1, device_id={"lat": south}, device_id_type=MESH)

    @pl.when(has_north)
    def _():
        pl.semaphore_signal(barrier, inc=1, device_id={"lat": north}, device_id_type=MESH)

    def pack(step):
        def body(q, _):
            base = pl.multiple_of((q // 4) * 256 + ((q // 2) % 2) * 128 + (q % 2) * 8, 8)
            parts = [shard[step, pl.ds(base + 16 * r, 8), :] for r in range(8)]
            gath[step, grp, pl.ds(pl.multiple_of(q * 8, 8), 8), :] = jnp.concatenate(parts, axis=1)
            return 0

        lax.fori_loop(0, 12, body, 0)

    def send_gath(step):
        for d, peer in enumerate(peers):
            remote(
                gath.at[step, grp], gath.at[step, grp],
                gath_send.at[step, d], gath_recv.at[step, d], {"grp": peer},
            ).start()

    loads[0].wait()
    pack(0)
    loads[2].wait()
    cols = [shard[s, pl.ds(8 * jb, 8), :] for s in range(2) for jb in range(2)]
    rows = [shard[s, pl.ds(256 + 128 * ib, 8, stride=16), :] for s in range(2) for ib in range(2)]
    near[0] = jnp.concatenate(cols + rows, axis=1)

    pl.semaphore_wait(barrier, groups + 1 + jnp.minimum(lat, 1) + jnp.minimum(lats - 1 - lat, 1))

    to_west = remote(near.at[0], near.at[1], near_send.at[0], near_recv.at[0], {"lon": west})
    to_south = remote(near.at[0], near.at[2], near_send.at[1], near_recv.at[1], {"lat": south})
    to_west.start()

    @pl.when(has_south)
    def _():
        to_south.start()

    send_gath(0)

    loads[1].wait()

    def turn(j, _):
        for i in range(16):
            field[0, j + 2, i + 2] = start[pl.ds(i * 16 + j, 8, stride=256), :]
        return 0

    lax.fori_loop(0, 16, turn, 0)

    for s in range(2):
        @pl.when(jnp.logical_not(has_south))
        def _():
            field[s, 0:2] = jnp.zeros((2, 20, 8, LANES), jnp.float32)

        @pl.when(jnp.logical_not(has_north))
        def _():
            field[s, 18:20] = jnp.zeros((2, 20, 8, LANES), jnp.float32)

    halo_west = remote(
        field.at[0, pl.ds(2, 16), pl.ds(2, 2)], field.at[0, pl.ds(2, 16), pl.ds(18, 2)],
        halo_send.at[0], halo_recv.at[0], {"lon": west},
    )
    halo_east = remote(
        field.at[0, pl.ds(2, 16), pl.ds(16, 2)], field.at[0, pl.ds(2, 16), pl.ds(0, 2)],
        halo_send.at[1], halo_recv.at[1], {"lon": east},
    )

    def lat_copies(step, send, recv):
        to_s = remote(
            field.at[step, pl.ds(2, 2), pl.ds(2, 16)], field.at[step, pl.ds(18, 2), pl.ds(2, 16)],
            send.at[0], recv.at[0], {"lat": south},
        )
        to_n = remote(
            field.at[step, pl.ds(16, 2), pl.ds(2, 16)], field.at[step, pl.ds(0, 2), pl.ds(2, 16)],
            send.at[1], recv.at[1], {"lat": north},
        )
        return to_s, to_n

    halo_south, halo_north = lat_copies(0, halo_send.at[pl.ds(2, 2)], halo_recv.at[pl.ds(2, 2)])
    halo_west.start()
    halo_east.start()

    @pl.when(has_south)
    def _():
        halo_south.start()

    @pl.when(has_north)
    def _():
        halo_north.start()

    to_west.wait_recv()

    @pl.when(has_north)
    def _():
        to_south.wait_recv()
        ext[grp] = jnp.where(lane < 64, near[1], near[2])

    @pl.when(jnp.logical_not(has_north))
    def _():
        ext[grp] = jnp.where(lane < 64, near[1], 0.0)

    for d, peer in enumerate(peers):
        remote(ext.at[grp], ext.at[grp], ext_send.at[d], ext_recv.at[d], {"grp": peer}).start()

    pack(1)
    send_gath(1)

    loads[4].wait()
    for s in range(2):
        def halve(j, _):
            full = given[s, j]
            high = full.astype(jnp.bfloat16)
            low = (full - high.astype(jnp.float32)).astype(jnp.bfloat16)
            for top in (0, 128):
                weights[s, j, top:top + 128, 0:128] = high
                weights[s, j, top:top + 128, 128:256] = low
            return 0

        lax.fori_loop(0, 16, halve, 0)

    loads[3].wait()
    first_row = lat * 16
    last_row = lats * 16

    def prepare(step):
        def unpack(q, _):
            rows = pl.ds(pl.multiple_of(q * 8, 8), 8)
            full = block_transpose([gath[step, g, rows, :] for g in range(8)], lane)
            at = pl.multiple_of((q % 2) * 8, 8)
            for r in range(8):
                courant[q // 4, ((q // 2) % 2) * 8 + r, pl.ds(at, 8), :] = full[r]
            return 0

        lax.fori_loop(0, 12, unpack, 0)
        edges = block_transpose([ext[g] for g in range(8)], lane)
        for jb in range(2):
            courant[0, 16, 8 * jb:8 * jb + 8, :] = edges[2 * step + jb]
        for ib in range(2):
            values = edges[4 + 2 * step + ib]
            for r in range(8):
                courant[1, 8 * ib + r, 16:17, :] = values[r:r + 1]

        def column(i, _):
            for jb in range(2):
                here = pl.ds(8 * jb, 8)
                w2, w1, lon0, e1, e2 = spread(faces(courant[0, i, here, :]), faces(courant[0, i + 1, here, :]))
                row = first_row + 8 * jb + sub

                def lat_faces(v, face_row):
                    v = jnp.where((face_row == 0) | (face_row == last_row), 0.0, v)
                    return faces(v, (face_row == 1) | (face_row == last_row - 1))

                s2, s1, lat0, n1, n2 = spread(
                    lat_faces(courant[1, i, here, :], row),
                    lat_faces(courant[1, i, pl.ds(8 * jb + 1, 8), :], row + 1),
                )
                up = jnp.where(lane == 0, 0.0, courant[2, i, here, :])
                low = faces(up, (lane == 1) | (lane == LANES - 1) | (lim[step, i, here, :] == 1))
                high = [pltpu.roll(x, LANES - 1, 1) for x in low]
                d2, d1, ver0, u1, u2 = spread(low, high)
                every = (1.0 + lon0 + lat0 + ver0, w2, w1, e1, e2, s2, s1, n1, n2, d2, d1, u1, u2)
                for n, value in enumerate(every):
                    coef[n, i, here, :] = value
            return 0

        lax.fori_loop(0, 16, column, 0)

    def advance(step, j, write):
        mid = [field[step, j + 2, i] for i in range(20)]
        for pair in range(8):
            new = []
            for i in (2 * pair, 2 * pair + 1):
                c = [jnp.broadcast_to(coef[n, i, pl.ds(j, 1), :], (8, LANES)) for n in range(POINTS)]
                q = mid[i + 2]
                lon_part = c[1] * mid[i] + c[2] * mid[i + 1] + c[3] * mid[i + 3] + c[4] * mid[i + 4]
                lat_part = (
                    c[5] * field[step, j, i + 2] + c[6] * field[step, j + 1, i + 2]
                    + c[7] * field[step, j + 3, i + 2] + c[8] * field[step, j + 4, i + 2]
                )
                ver_part = (
                    c[9] * pltpu.roll(q, 2, 1) + c[10] * pltpu.roll(q, 1, 1)
                    + c[11] * pltpu.roll(q, LANES - 1, 1) + c[12] * pltpu.roll(q, LANES - 2, 1)
                )
                new.append(c[0] * q + lon_part + (lat_part + ver_part))
            both = jnp.concatenate(new, axis=0)
            high = both.astype(jnp.bfloat16)
            split[16 * pair:16 * pair + 16, 0:128] = high
            split[16 * pair:16 * pair + 16, 128:256] = (both - high.astype(jnp.float32)).astype(jnp.bfloat16)
        product = jnp.dot(split[...], weights[step, j], preferred_element_type=jnp.float32)
        total = product[:, 0:128] + product[:, 128:256]
        for i in range(16):
            write(j, i, total[8 * i:8 * i + 8])

    for d, peer in enumerate(peers):
        remote(ext.at[grp], ext.at[grp], ext_send.at[d], ext_recv.at[d], {"grp": peer}).wait()
        remote(
            gath.at[0, grp], gath.at[0, grp], gath_send.at[0, d], gath_recv.at[0, d], {"grp": peer}
        ).wait()
    prepare(0)

    halo_west.wait()
    halo_east.wait()

    @pl.when(has_south)
    def _():
        halo_south.wait_send()
        halo_north.wait_recv()

    @pl.when(has_north)
    def _():
        halo_north.wait_send()
        halo_south.wait_recv()

    def lon_copies(chunk):
        rows = pl.ds(chunk * 4 + 2, 4)
        to_w = remote(
            field.at[1, rows, pl.ds(2, 2)], field.at[1, rows, pl.ds(18, 2)],
            lon_send.at[0, chunk], lon_recv.at[0, chunk], {"lon": west},
        )
        to_e = remote(
            field.at[1, rows, pl.ds(16, 2)], field.at[1, rows, pl.ds(0, 2)],
            lon_send.at[1, chunk], lon_recv.at[1, chunk], {"lon": east},
        )
        return to_w, to_e

    next_south, next_north = lat_copies(1, lat_send, lat_recv)

    def first_write(j, i, value):
        field[1, j + 2, i + 2] = value

    def first_chunk(n, _):
        chunk = (3 * n) % 4

        def row(r, _):
            advance(0, chunk * 4 + r, first_write)
            return 0

        lax.fori_loop(0, 4, row, 0)
        for copy in lon_copies(chunk):
            copy.start()

        @pl.when(jnp.logical_and(n == 0, has_south))
        def _():
            next_south.start()

        @pl.when(jnp.logical_and(n == 1, has_north))
        def _():
            next_north.start()

        return 0

    lax.fori_loop(0, 4, first_chunk, 0)

    for d, peer in enumerate(peers):
        remote(
            gath.at[1, grp], gath.at[1, grp], gath_send.at[1, d], gath_recv.at[1, d], {"grp": peer}
        ).wait()
    prepare(1)

    @pl.when(has_south)
    def _():
        next_south.wait_send()
        next_north.wait_recv()

    @pl.when(has_north)
    def _():
        next_north.wait_send()
        next_south.wait_recv()

    def second_write(j, i, value):
        done[pl.ds(i * 16 + j, 8, stride=256), :] = value

    def second_chunk(n, _):
        chunk = (3 * n) % 4
        for copy in lon_copies(chunk):
            copy.wait()

        def row(r, _):
            advance(1, chunk * 4 + r, second_write)
            return 0

        lax.fori_loop(0, 4, row, 0)
        return 0

    lax.fori_loop(0, 4, second_chunk, 0)
    to_west.wait_send()

    @pl.when(has_south)
    def _():
        to_south.wait_send()

    result = pltpu.make_async_copy(done, out, out_sem)
    result.start()
    result.wait()


def on_device(tracers, fluxes, limiter_mask, diffusion_inverse):
    f32 = jnp.float32
    dma = pltpu.SemaphoreType.DMA
    out = pl.pallas_call(
        kernel,
        out_shape=jax.ShapeDtypeStruct((2048, LANES), f32),
        in_specs=[pl.BlockSpec(memory_space=pl.ANY)] * 4,
        out_specs=pl.BlockSpec(memory_space=pl.ANY),
        scratch_shapes=[
            pltpu.VMEM((2, 768, 16), f32),
            pltpu.VMEM((2, 8, 96, LANES), f32),
            pltpu.VMEM((3, 8, LANES), f32),
            pltpu.VMEM((8, 8, LANES), f32),
            pltpu.VMEM((2048, LANES), f32),
            pltpu.VMEM((2, 20, 20, 8, LANES), f32),
            pltpu.VMEM((2, 16, 128, 128), f32),
            pltpu.VMEM((2, 16, 256, 256), jnp.bfloat16),
            pltpu.VMEM((POINTS, 16, 16, LANES), f32),
            pltpu.VMEM((3, 17, 24, LANES), f32),
            pltpu.VMEM((2, 16, 16, LANES), jnp.int32),
            pltpu.VMEM((128, 256), jnp.bfloat16),
            pltpu.VMEM((2048, LANES), f32),
            dma((5,)), dma,
            dma((2,)), dma((2,)),
            dma((7,)), dma((7,)),
            dma((2, 7)), dma((2, 7)),
            dma((4,)), dma((4,)),
            dma((2, 4)), dma((2, 4)),
            dma((2,)), dma((2,)),
        ],
        compiler_params=pltpu.CompilerParams(
            collective_id=0, has_side_effects=True, vmem_limit_bytes=40 * 1024 * 1024
        ),
        name="transport",
    )(
        tracers.reshape(2048, LANES), fluxes.reshape(2, 768, 16), limiter_mask, diffusion_inverse
    )
    return out.reshape(8, 16, 16, LANES)


def solution(mesh):
    in_specs = (
        P("grp", "lon", "lat", None),
        P(None, None, "lon", "lat", "grp"),
        P(None, "lon", "lat", None),
        P(None, "lat", None, None),
    )
    out_specs = P("grp", "lon", "lat", None)
    return jax.shard_map(
        on_device, mesh=mesh, in_specs=in_specs, out_specs=out_specs, check_vma=False
    )
```

time: 200 us -> 48.6 us (0.24)
  blocking collectives: 126 us -> 0 us
  Pallas kernels: 0 us -> 42 us
  starting transfers between devices: 32.4 us -> 0 us
  local copies, waits for them, and re-layouts: 23.8 us -> 5.87 us
  other arithmetic: 11.3 us -> 0 us
  matrix products: 5.29 us -> 0 us
    all_gather x1 -> x0, blocking collectives: 126 us -> none  [on_device(): gathered = lax.all_gather(fluxes, 'grp', axis=4, tiled=True)]
    pallas_call x0 -> x1, Pallas kernels: none -> 42 us  [on_device(): pl.pallas_call(kernel, out_shape=jax.ShapeDtypeStruct((2048, LANES), f32)...]
    ppermute x8 -> x0, starting transfers between devices: 32.4 us -> none  [the longest x4 21.8 us: padded_2(): after = lax.ppermute(leading, axis, down)]
    dot_general x2 -> x0, matrix products: 5.29 us -> none  [diffuse(): jnp.einsum('jzk,tijk->tijz', inverse_rows, current, precision=lax.Precisi...]
    mul x3 -> x0, local copies, waits for them, and re-layouts: 4.84 us -> none  [first_order(): courant * (plus_zero + minus_one) / 2.0]
    unnamed x16 -> x9, local copies, waits for them, and re-layouts: 9.96 us -> 5.87 us
    slice x3 -> x0, local copies, waits for them, and re-layouts: 3.53 us -> none  [the longest x1 2.86 us: advect(): joined = jnp.concatenate([current, step_flux[0:2]], axis=0)]
    select_n x4 -> x0, other arithmetic: 3.32 us -> none  [the longest x2 1.81 us: vertical_change(): jnp.where(level_idx == 0, 0.0, jnp.where((level_idx == 1) | (level_idx ==...]
  transfers between devices with their start and end apart: 8 -> 0, of which waited for: 1 -> 0; matrix products, arithmetic and copies ran while one was open for 10% -> 0% of each run, Pallas kernels for 0% -> 0%
where the time goes in v1:
time: 48.6 us; the launch traced here: 47.9 us
  Pallas kernels  42 us (86%)
  local copies, waits for them, and re-layouts  5.87 us (12%)
    pallas_call x1, Pallas kernels, on_device(): pl.pallas_call(kernel, out_shape=jax.ShapeDtypeStruct((2048, LANES), f32)...  42 us
    unnamed x9, local copies, waits for them, and re-layouts  5.87 us

profile of v1, /device:TPU:1, one launch (start us, length us, event | category | flops | bytes accessed | tf_op | source)
XLA Modules:
  0.0 47.9 jit_solution(16649155586151581711)
XLA Ops:
  0.0 0.0 copy-start
  0.0 1.6 %copy-done = f32[2,16,128,128]{3,2,1,0:T(8,128)S(1)} copy-done((f32[2,16,128,128]{3,2,1,0:T(8,128)S(1)}, f32[2,16,128,128]{3,2,1,0:T(8,128)}, u32[]{:S(2)}) %copy-start) | copy-done | bytes 2097176
  1.6 0.0 copy-start.1
  1.6 1.2 %copy-done.1 = f32[8,16,16,128]{3,2,1,0:T(8,128)S(1)} copy-done((f32[8,16,16,128]{3,2,1,0:T(8,128)S(1)}, f32[8,16,16,128]{3,2,1,0:T(8,128)}, u32[]{:S(2)}) %copy-start.1) | copy-done | bytes 1048600
  2.8 0.0 copy-start.2
  2.8 1.1 %copy-done.2 = f32[2,3,16,16,16]{4,3,2,1,0:T(8,128)S(1)} copy-done((f32[2,3,16,16,16]{4,3,2,1,0:T(8,128)S(1)}, f32[2,3,16,16,16]{4,3,2,1,0:T(8,128)}, u32[]{:S(2)}) %copy-start.2) | copy-done | bytes 98328
  4.0 0.0 copy-start.3
  4.0 0.9 %copy-done.3 = s32[2,16,16,128]{3,2,1,0:T(8,128)S(1)} copy-done((s32[2,16,16,128]{3,2,1,0:T(8,128)S(1)}, s32[2,16,16,128]{3,2,1,0:T(8,128)}, u32[]{:S(2)}) %copy-start.3) | copy-done | bytes 262168
  4.9 42.0 %transport.1 = f32[2048,128]{1,0:T(8,128)S(1)} custom-call(f32[2048,128]{1,0:T(8,128)S(1)} %bitcast.4, f32[2,768,16]{2,1,0:T(8,128)S(1)} %bitcast.5, s32[2,16,16,128]{3,2,1,0:T(8,128)S(1)} %copy-done.3, f32[2,16,128,128]{3,2,1,0:T(8,128)S(1)} %copy-done), custom_call_target="tpu_custom_call" | custom-call | tf_op jit(solution)/shard_map/transport/pallas_call | solution.py:383
  46.9 1.0 %copy.6 = f32[8,16,16,128]{3,2,1,0:T(8,128)} copy(f32[8,16,16,128]{3,2,1,0:T(8,128)S(1)} %bitcast.3) | data formatting | bytes 2097152
Async XLA Ops:
  0.0 1.6 %copy-start = (f32[2,16,128,128]{3,2,1,0:T(8,128)S(1)}, f32[2,16,128,128]{3,2,1,0:T(8,128)}, u32[]{:S(2)}) copy-start(f32[2,16,128,128]{3,2,1,0:T(8,128)} %inverse.1) | copy-start | bytes 6291460
  1.6 1.2 %copy-start.1 = (f32[8,16,16,128]{3,2,1,0:T(8,128)S(1)}, f32[8,16,16,128]{3,2,1,0:T(8,128)}, u32[]{:S(2)}) copy-start(f32[8,16,16,128]{3,2,1,0:T(8,128)} %param.4) | copy-start | bytes 3145732
  2.8 1.1 %copy-start.2 = (f32[2,3,16,16,16]{4,3,2,1,0:T(8,128)S(1)}, f32[2,3,16,16,16]{4,3,2,1,0:T(8,128)}, u32[]{:S(2)}) copy-start(f32[2,3,16,16,16]{4,3,2,1,0:T(8,128)} %param.5) | copy-start | bytes 294916
  4.0 0.9 %copy-start.3 = (s32[2,16,16,128]{3,2,1,0:T(8,128)S(1)}, s32[2,16,16,128]{3,2,1,0:T(8,128)}, u32[]{:S(2)}) copy-start(s32[2,16,16,128]{3,2,1,0:T(8,128)} %limiter.1) | copy-start | bytes 786436

commit v2 on v1

--- a/solution.py
+++ b/solution.py
@@ -43,8 +43,8 @@
 
 def kernel(
     tracers, fluxes, limiter, inverse, out,
-    shard, gath, near, ext, start, field, given, weights, coef, courant, lim, split, done,
-    in_sem, out_sem, near_send, near_recv, ext_send, ext_recv, gath_send, gath_recv,
+    shard, gath, near, ext, start, field0, field1, given, weights, coef, courant, lim,
+    even_split, odd_split, done, in_sem, out_sem, near_send, near_recv, ext_send, ext_recv, gath_send, gath_recv,
     halo_send, halo_recv, lon_send, lon_recv, lat_send, lat_recv,
 ):
     groups, lons, lats = lax.axis_size("grp"), lax.axis_size("lon"), lax.axis_size("lat")
@@ -87,13 +87,15 @@
         pl.semaphore_signal(barrier, inc=1, device_id={"lat": north}, device_id_type=MESH)
 
     def pack(step):
-        def body(q, _):
-            base = pl.multiple_of((q // 4) * 256 + ((q // 2) % 2) * 128 + (q % 2) * 8, 8)
-            parts = [shard[step, pl.ds(base + 16 * r, 8), :] for r in range(8)]
-            gath[step, grp, pl.ds(pl.multiple_of(q * 8, 8), 8), :] = jnp.concatenate(parts, axis=1)
+        def body(c, _):
+            for q in range(4):
+                base = pl.multiple_of(c * 256 + (q // 2) * 128 + (q % 2) * 8, 8)
+                parts = [shard[step, pl.ds(base + 16 * r, 8), :] for r in range(8)]
+                rows = pl.ds(pl.multiple_of(c * 32 + q * 8, 8), 8)
+                gath[step, grp, rows, :] = jnp.concatenate(parts, axis=1)
             return 0
 
-        lax.fori_loop(0, 12, body, 0)
+        lax.fori_loop(0, 3, body, 0)
 
     def send_gath(step):
         for d, peer in enumerate(peers):
@@ -125,41 +127,41 @@
 
     def turn(j, _):
         for i in range(16):
-            field[0, j + 2, i + 2] = start[pl.ds(i * 16 + j, 8, stride=256), :]
+            field0[j + 2, i + 2] = start[pl.ds(i * 16 + j, 8, stride=256), :]
         return 0
 
     lax.fori_loop(0, 16, turn, 0)
 
-    for s in range(2):
+    for field in (field0, field1):
         @pl.when(jnp.logical_not(has_south))
         def _():
-            field[s, 0:2] = jnp.zeros((2, 20, 8, LANES), jnp.float32)
+            field[0:2] = jnp.zeros((2, 20, 8, LANES), jnp.float32)
 
         @pl.when(jnp.logical_not(has_north))
         def _():
-            field[s, 18:20] = jnp.zeros((2, 20, 8, LANES), jnp.float32)
+            field[18:20] = jnp.zeros((2, 20, 8, LANES), jnp.float32)
 
     halo_west = remote(
-        field.at[0, pl.ds(2, 16), pl.ds(2, 2)], field.at[0, pl.ds(2, 16), pl.ds(18, 2)],
+        field0.at[pl.ds(2, 16), pl.ds(2, 2)], field0.at[pl.ds(2, 16), pl.ds(18, 2)],
         halo_send.at[0], halo_recv.at[0], {"lon": west},
     )
     halo_east = remote(
-        field.at[0, pl.ds(2, 16), pl.ds(16, 2)], field.at[0, pl.ds(2, 16), pl.ds(0, 2)],
+        field0.at[pl.ds(2, 16), pl.ds(16, 2)], field0.at[pl.ds(2, 16), pl.ds(0, 2)],
         halo_send.at[1], halo_recv.at[1], {"lon": east},
     )
 
-    def lat_copies(step, send, recv):
+    def lat_copies(field, send, recv):
         to_s = remote(
-            field.at[step, pl.ds(2, 2), pl.ds(2, 16)], field.at[step, pl.ds(18, 2), pl.ds(2, 16)],
+            field.at[pl.ds(2, 2), pl.ds(2, 16)], field.at[pl.ds(18, 2), pl.ds(2, 16)],
             send.at[0], recv.at[0], {"lat": south},
         )
         to_n = remote(
-            field.at[step, pl.ds(16, 2), pl.ds(2, 16)], field.at[step, pl.ds(0, 2), pl.ds(2, 16)],
+            field.at[pl.ds(16, 2), pl.ds(2, 16)], field.at[pl.ds(0, 2), pl.ds(2, 16)],
             send.at[1], recv.at[1], {"lat": north},
         )
         return to_s, to_n
 
-    halo_south, halo_north = lat_copies(0, halo_send.at[pl.ds(2, 2)], halo_recv.at[pl.ds(2, 2)])
+    halo_south, halo_north = lat_copies(field0, halo_send.at[pl.ds(2, 2)], halo_recv.at[pl.ds(2, 2)])
     halo_west.start()
     halo_east.start()
 
@@ -206,15 +208,15 @@
     last_row = lats * 16
 
     def prepare(step):
-        def unpack(q, _):
-            rows = pl.ds(pl.multiple_of(q * 8, 8), 8)
-            full = block_transpose([gath[step, g, rows, :] for g in range(8)], lane)
-            at = pl.multiple_of((q % 2) * 8, 8)
-            for r in range(8):
-                courant[q // 4, ((q // 2) % 2) * 8 + r, pl.ds(at, 8), :] = full[r]
+        def unpack(c, _):
+            for q in range(4):
+                rows = pl.ds(pl.multiple_of(c * 32 + q * 8, 8), 8)
+                full = block_transpose([gath[step, g, rows, :] for g in range(8)], lane)
+                for r in range(8):
+                    courant[c, (q // 2) * 8 + r, 8 * (q % 2):8 * (q % 2) + 8, :] = full[r]
             return 0
 
-        lax.fori_loop(0, 12, unpack, 0)
+        lax.fori_loop(0, 3, unpack, 0)
         edges = block_transpose([ext[g] for g in range(8)], lane)
         for jb in range(2):
             courant[0, 16, 8 * jb:8 * jb + 8, :] = edges[2 * step + jb]
@@ -223,33 +225,37 @@
             for r in range(8):
                 courant[1, 8 * ib + r, 16:17, :] = values[r:r + 1]
 
-        def column(i, _):
+        def lat_faces(v, face_row):
+            v = jnp.where((face_row == 0) | (face_row == last_row), 0.0, v)
+            return faces(v, (face_row == 1) | (face_row == last_row - 1))
+
+        def columns(n, _):
             for jb in range(2):
                 here = pl.ds(8 * jb, 8)
-                w2, w1, lon0, e1, e2 = spread(faces(courant[0, i, here, :]), faces(courant[0, i + 1, here, :]))
                 row = first_row + 8 * jb + sub
-
-                def lat_faces(v, face_row):
-                    v = jnp.where((face_row == 0) | (face_row == last_row), 0.0, v)
-                    return faces(v, (face_row == 1) | (face_row == last_row - 1))
-
-                s2, s1, lat0, n1, n2 = spread(
-                    lat_faces(courant[1, i, here, :], row),
-                    lat_faces(courant[1, i, pl.ds(8 * jb + 1, 8), :], row + 1),
-                )
-                up = jnp.where(lane == 0, 0.0, courant[2, i, here, :])
-                low = faces(up, (lane == 1) | (lane == LANES - 1) | (lim[step, i, here, :] == 1))
-                high = [pltpu.roll(x, LANES - 1, 1) for x in low]
-                d2, d1, ver0, u1, u2 = spread(low, high)
-                every = (1.0 + lon0 + lat0 + ver0, w2, w1, e1, e2, s2, s1, n1, n2, d2, d1, u1, u2)
-                for n, value in enumerate(every):
-                    coef[n, i, here, :] = value
+                western = faces(courant[0, n * 4, here, :])
+                for more in range(4):
+                    i = n * 4 + more
+                    eastern = faces(courant[0, i + 1, here, :])
+                    w2, w1, lon0, e1, e2 = spread(western, eastern)
+                    western = eastern
+                    s2, s1, lat0, n1, n2 = spread(
+                        lat_faces(courant[1, i, here, :], row),
+                        lat_faces(courant[1, i, pl.ds(8 * jb + 1, 8), :], row + 1),
+                    )
+                    up = jnp.where(lane == 0, 0.0, courant[2, i, here, :])
+                    low = faces(up, (lane == 1) | (lane == LANES - 1) | (lim[step, i, here, :] == 1))
+                    high = [pltpu.roll(x, LANES - 1, 1) for x in low]
+                    d2, d1, ver0, u1, u2 = spread(low, high)
+                    every = (1.0 + lon0 + lat0 + ver0, w2, w1, e1, e2, s2, s1, n1, n2, d2, d1, u1, u2)
+                    for point, value in enumerate(every):
+                        coef[point, i, here, :] = value
             return 0
 
-        lax.fori_loop(0, 16, column, 0)
-
-    def advance(step, j, write):
-        mid = [field[step, j + 2, i] for i in range(20)]
+        lax.fori_loop(0, 4, columns, 0)
+
+    def stencil(field, j, split):
+        mid = [field[j + 2, i] for i in range(20)]
         for pair in range(8):
             new = []
             for i in (2 * pair, 2 * pair + 1):
@@ -257,8 +263,8 @@
                 q = mid[i + 2]
                 lon_part = c[1] * mid[i] + c[2] * mid[i + 1] + c[3] * mid[i + 3] + c[4] * mid[i + 4]
                 lat_part = (
-                    c[5] * field[step, j, i + 2] + c[6] * field[step, j + 1, i + 2]
-                    + c[7] * field[step, j + 3, i + 2] + c[8] * field[step, j + 4, i + 2]
+                    c[5] * field[j, i + 2] + c[6] * field[j + 1, i + 2]
+                    + c[7] * field[j + 3, i + 2] + c[8] * field[j + 4, i + 2]
                 )
                 ver_part = (
                     c[9] * pltpu.roll(q, 2, 1) + c[10] * pltpu.roll(q, 1, 1)
@@ -269,10 +275,27 @@
             high = both.astype(jnp.bfloat16)
             split[16 * pair:16 * pair + 16, 0:128] = high
             split[16 * pair:16 * pair + 16, 128:256] = (both - high.astype(jnp.float32)).astype(jnp.bfloat16)
+
+    def diffuse(step, j, split, write):
         product = jnp.dot(split[...], weights[step, j], preferred_element_type=jnp.float32)
         total = product[:, 0:128] + product[:, 128:256]
         for i in range(16):
             write(j, i, total[8 * i:8 * i + 8])
+
+    def chunk_of(step, n):
+        if step == 0:
+            return (3 * n) % 4
+        late = n // 2
+        return late * (n - 2) + (1 - late) * (3 - n)
+
+    def row_of(step, n):
+        return chunk_of(step, n // 4) * 4 + n % 4
+
+    def two_rows(step, field, n, write):
+        diffuse(step, row_of(step, jnp.maximum(n - 1, 0)), odd_split, write)
+        stencil(field, row_of(step, n), even_split)
+        diffuse(step, row_of(step, n), even_split, write)
+        stencil(field, row_of(step, n + 1), odd_split)
 
     for d, peer in enumerate(peers):
         remote(ext.at[grp], ext.at[grp], ext_send.at[d], ext_recv.at[d], {"grp": peer}).wait()
@@ -297,42 +320,47 @@
     def lon_copies(chunk):
         rows = pl.ds(chunk * 4 + 2, 4)
         to_w = remote(
-            field.at[1, rows, pl.ds(2, 2)], field.at[1, rows, pl.ds(18, 2)],
+            field1.at[rows, pl.ds(2, 2)], field1.at[rows, pl.ds(18, 2)],
             lon_send.at[0, chunk], lon_recv.at[0, chunk], {"lon": west},
         )
         to_e = remote(
-            field.at[1, rows, pl.ds(16, 2)], field.at[1, rows, pl.ds(0, 2)],
+            field1.at[rows, pl.ds(16, 2)], field1.at[rows, pl.ds(0, 2)],
             lon_send.at[1, chunk], lon_recv.at[1, chunk], {"lon": east},
         )
         return to_w, to_e
 
-    next_south, next_north = lat_copies(1, lat_send, lat_recv)
+    next_south, next_north = lat_copies(field1, lat_send, lat_recv)
 
     def first_write(j, i, value):
-        field[1, j + 2, i + 2] = value
+        field1[j + 2, i + 2] = value
+
+    def give(n):
+        for copy in lon_copies(chunk_of(0, n)):
+            copy.start()
+
+        @pl.when(jnp.logical_and(n == 0, has_south))
+        def _():
+            next_south.start()
+
+        @pl.when(jnp.logical_and(n == 1, has_north))
+        def _():
+            next_north.start()
+
+    odd_split[...] = jnp.zeros((128, 256), jnp.bfloat16)
 
     def first_chunk(n, _):
-        chunk = (3 * n) % 4
-
-        def row(r, _):
-            advance(0, chunk * 4 + r, first_write)
-            return 0
-
-        lax.fori_loop(0, 4, row, 0)
-        for copy in lon_copies(chunk):
-            copy.start()
-
-        @pl.when(jnp.logical_and(n == 0, has_south))
-        def _():
-            next_south.start()
-
-        @pl.when(jnp.logical_and(n == 1, has_north))
-        def _():
-            next_north.start()
-
+        two_rows(0, field0, 4 * n, first_write)
+
+        @pl.when(n > 0)
+        def _():
+            give(n - 1)
+
+        two_rows(0, field0, 4 * n + 2, first_write)
         return 0
 
     lax.fori_loop(0, 4, first_chunk, 0)
+    diffuse(0, row_of(0, 15), odd_split, first_write)
+    give(3)
 
     for d, peer in enumerate(peers):
         remote(
@@ -350,31 +378,38 @@
         next_north.wait_send()
         next_south.wait_recv()
 
+    results = []
+    for half in range(2):
+        rows = pl.ds(8 * half, 8)
+        here = done.reshape(128, 16, LANES).at[:, rows]
+        results.append(pltpu.make_async_copy(here, out.at[:, rows], out_sem.at[half]))
+
     def second_write(j, i, value):
         done[pl.ds(i * 16 + j, 8, stride=256), :] = value
 
     def second_chunk(n, _):
-        chunk = (3 * n) % 4
-        for copy in lon_copies(chunk):
+        for copy in lon_copies(chunk_of(1, n)):
             copy.wait()
-
-        def row(r, _):
-            advance(1, chunk * 4 + r, second_write)
-            return 0
-
-        lax.fori_loop(0, 4, row, 0)
+        two_rows(1, field1, 4 * n, second_write)
+
+        @pl.when(n == 2)
+        def _():
+            results[1].start()
+
+        two_rows(1, field1, 4 * n + 2, second_write)
         return 0
 
     lax.fori_loop(0, 4, second_chunk, 0)
+    diffuse(1, row_of(1, 15), odd_split, second_write)
+    results[0].start()
     to_west.wait_send()
 
     @pl.when(has_south)
     def _():
         to_south.wait_send()
 
-    result = pltpu.make_async_copy(done, out, out_sem)
-    result.start()
-    result.wait()
+    for result in results:
+        result.wait()
 
 
 def on_device(tracers, fluxes, limiter_mask, diffusion_inverse):
@@ -382,7 +417,7 @@
     dma = pltpu.SemaphoreType.DMA
     out = pl.pallas_call(
         kernel,
-        out_shape=jax.ShapeDtypeStruct((2048, LANES), f32),
+        out_shape=jax.ShapeDtypeStruct((128, 16, LANES), f32),
         in_specs=[pl.BlockSpec(memory_space=pl.ANY)] * 4,
         out_specs=pl.BlockSpec(memory_space=pl.ANY),
         scratch_shapes=[
@@ -391,15 +426,17 @@
             pltpu.VMEM((3, 8, LANES), f32),
             pltpu.VMEM((8, 8, LANES), f32),
             pltpu.VMEM((2048, LANES), f32),
-            pltpu.VMEM((2, 20, 20, 8, LANES), f32),
+            pltpu.VMEM((20, 20, 8, LANES), f32),
+            pltpu.VMEM((20, 20, 8, LANES), f32),
             pltpu.VMEM((2, 16, 128, 128), f32),
             pltpu.VMEM((2, 16, 256, 256), jnp.bfloat16),
             pltpu.VMEM((POINTS, 16, 16, LANES), f32),
             pltpu.VMEM((3, 17, 24, LANES), f32),
             pltpu.VMEM((2, 16, 16, LANES), jnp.int32),
             pltpu.VMEM((128, 256), jnp.bfloat16),
+            pltpu.VMEM((128, 256), jnp.bfloat16),
             pltpu.VMEM((2048, LANES), f32),
-            dma((5,)), dma,
+            dma((5,)), dma((2,)),
             dma((2,)), dma((2,)),
             dma((7,)), dma((7,)),
             dma((2, 7)), dma((2, 7)),
@@ -408,7 +445,7 @@
             dma((2,)), dma((2,)),
         ],
         compiler_params=pltpu.CompilerParams(
-            collective_id=0, has_side_effects=True, vmem_limit_bytes=40 * 1024 * 1024
+            collective_id=0, has_side_effects=True, vmem_limit_bytes=58 * 1024 * 1024
         ),
         name="transport",
     )(

time: 48.6 us -> 38.4 us (0.79); the launches traced: 47.9 us -> 38.3 us
  Pallas kernels: 42 us -> 36 us
  local copies, waits for them, and re-layouts: 5.87 us -> 2.27 us
    pallas_call x1, Pallas kernels: 42 us -> 36 us  [on_device(): pl.pallas_call(kernel, out_shape=jax.ShapeDtypeStruct((128, 16, LANES), f...]
    unnamed x9 -> x1, local copies, waits for them, and re-layouts: 5.87 us -> 2.27 us
where the time goes in v2:
time: 38.4 us; the launch traced here: 38.3 us
  Pallas kernels  36 us (94%)
  local copies, waits for them, and re-layouts  2.27 us (6%)
    pallas_call x1, Pallas kernels, on_device(): pl.pallas_call(kernel, out_shape=jax.ShapeDtypeStruct((128, 16, LANES), f...  36 us
    unnamed x1, local copies, waits for them, and re-layouts  2.27 us

profile of v2, /device:TPU:1, one launch (start us, length us, event | category | flops | bytes accessed | tf_op | source)
XLA Modules:
  0.0 38.3 jit_solution(2667294524850669434)
XLA Ops:
  0.0 36.0 %transport.1 = f32[128,16,128]{2,1,0:T(8,128)} custom-call(f32[2048,128]{1,0:T(8,128)} %bitcast.4, f32[2,768,16]{2,1,0:T(8,128)} %bitcast.5, s32[2,16,16,128]{3,2,1,0:T(8,128)} %limiter.1, f32[2,16,128,128]{3,2,1,0:T(8,128)} %inverse.1), custom_call_target="tpu_custom_call" | custom-call | tf_op jit(solution)/shard_map/transport/pallas_call | solution.py:418
  36.0 2.3 %copy.6 = f32[8,16,16,128]{3,2,1,0:T(8,128)} copy(f32[8,16,16,128]{3,2,1,0:T(8,128)} %bitcast.3) | data formatting | bytes 2097152

commit v3 on v2

--- a/solution.py
+++ b/solution.py
@@ -52,7 +52,10 @@
     east, west = lax.rem(lon + 1, lons), lax.rem(lon + lons - 1, lons)
     has_south, has_north = lat > 0, lat < lats - 1
     south, north = lat - 1, lat + 1
-    peers = [lax.rem(grp + d, groups) for d in range(1, groups)]
+    peers = [
+        lax.rem(grp // 2 + dx, groups // 2) * 2 + lax.rem(grp + dy, 2)
+        for dx, dy in ((2, 1), (1, 1), (3, 1), (2, 0), (0, 1), (1, 0), (3, 0))
+    ]
     lane = lax.broadcasted_iota(jnp.int32, (8, LANES), 1)
     sub = lax.broadcasted_iota(jnp.int32, (8, LANES), 0)
 
@@ -64,8 +67,8 @@
 
     loads = [
         pltpu.make_async_copy(fluxes.at[0], shard.at[0], in_sem.at[0]),
-        pltpu.make_async_copy(tracers, start, in_sem.at[1]),
-        pltpu.make_async_copy(fluxes.at[1], shard.at[1], in_sem.at[2]),
+        pltpu.make_async_copy(fluxes.at[1], shard.at[1], in_sem.at[1]),
+        pltpu.make_async_copy(tracers, start, in_sem.at[2]),
         pltpu.make_async_copy(limiter, lim, in_sem.at[3]),
         pltpu.make_async_copy(inverse, given, in_sem.at[4]),
     ]
@@ -104,26 +107,15 @@
                 gath_send.at[step, d], gath_recv.at[step, d], {"grp": peer},
             ).start()
 
-    loads[0].wait()
-    pack(0)
-    loads[2].wait()
+    for step in range(2):
+        loads[step].wait()
+        pack(step)
     cols = [shard[s, pl.ds(8 * jb, 8), :] for s in range(2) for jb in range(2)]
     rows = [shard[s, pl.ds(256 + 128 * ib, 8, stride=16), :] for s in range(2) for ib in range(2)]
     near[0] = jnp.concatenate(cols + rows, axis=1)
 
-    pl.semaphore_wait(barrier, groups + 1 + jnp.minimum(lat, 1) + jnp.minimum(lats - 1 - lat, 1))
-
-    to_west = remote(near.at[0], near.at[1], near_send.at[0], near_recv.at[0], {"lon": west})
-    to_south = remote(near.at[0], near.at[2], near_send.at[1], near_recv.at[1], {"lat": south})
-    to_west.start()
-
-    @pl.when(has_south)
-    def _():
-        to_south.start()
-
-    send_gath(0)
-
-    loads[1].wait()
+
+    loads[2].wait()
 
     def turn(j, _):
         for i in range(16):
@@ -140,6 +132,16 @@
         @pl.when(jnp.logical_not(has_north))
         def _():
             field[18:20] = jnp.zeros((2, 20, 8, LANES), jnp.float32)
+
+    pl.semaphore_wait(barrier, groups + 1 + jnp.minimum(lat, 1) + jnp.minimum(lats - 1 - lat, 1))
+
+    to_west = remote(near.at[0], near.at[1], near_send.at[0], near_recv.at[0], {"lon": west})
+    to_south = remote(near.at[0], near.at[2], near_send.at[1], near_recv.at[1], {"lat": south})
+    to_west.start()
+
+    @pl.when(has_south)
+    def _():
+        to_south.start()
 
     halo_west = remote(
         field0.at[pl.ds(2, 16), pl.ds(2, 2)], field0.at[pl.ds(2, 16), pl.ds(18, 2)],
@@ -173,6 +175,8 @@
     def _():
         halo_north.start()
 
+    send_gath(0)
+
     to_west.wait_recv()
 
     @pl.when(has_north)
@@ -187,8 +191,6 @@
     for d, peer in enumerate(peers):
         remote(ext.at[grp], ext.at[grp], ext_send.at[d], ext_recv.at[d], {"grp": peer}).start()
 
-    pack(1)
-    send_gath(1)
 
     loads[4].wait()
     for s in range(2):
@@ -298,10 +300,15 @@
         stencil(field, row_of(step, n + 1), odd_split)
 
     for d, peer in enumerate(peers):
+        remote(
+            gath.at[0, grp], gath.at[0, grp], gath_send.at[0, d], gath_recv.at[0, d], {"grp": peer}
+        ).wait_send()
+    send_gath(1)
+    for d, peer in enumerate(peers):
         remote(ext.at[grp], ext.at[grp], ext_send.at[d], ext_recv.at[d], {"grp": peer}).wait()
         remote(
             gath.at[0, grp], gath.at[0, grp], gath_send.at[0, d], gath_recv.at[0, d], {"grp": peer}
-        ).wait()
+        ).wait_recv()
     prepare(0)
 
     halo_west.wait()

time: 38.4 us -> 36.3 us (0.945)
  Pallas kernels: 36 us -> 33.8 us
    pallas_call x1, Pallas kernels: 36 us -> 33.8 us  [on_device(): pl.pallas_call(kernel, out_shape=jax.ShapeDtypeStruct((128, 16, LANES), f...]
where the time goes in v3:
time: 36.3 us; the launch traced here: 36.1 us
  Pallas kernels  33.8 us (93%)
  local copies, waits for them, and re-layouts  2.27 us (6%)
    pallas_call x1, Pallas kernels, on_device(): pl.pallas_call(kernel, out_shape=jax.ShapeDtypeStruct((128, 16, LANES), f...  33.8 us
    unnamed x1, local copies, waits for them, and re-layouts  2.27 us

profile of v3, /device:TPU:1, one launch (start us, length us, event | category | flops | bytes accessed | tf_op | source)
XLA Modules:
  0.0 36.1 jit_solution(11961712772850719886)
XLA Ops:
  0.0 33.8 %transport.1 = f32[128,16,128]{2,1,0:T(8,128)} custom-call(f32[2048,128]{1,0:T(8,128)} %bitcast.4, f32[2,768,16]{2,1,0:T(8,128)} %bitcast.5, s32[2,16,16,128]{3,2,1,0:T(8,128)} %limiter.1, f32[2,16,128,128]{3,2,1,0:T(8,128)} %inverse.1), custom_call_target="tpu_custom_call" | custom-call | tf_op jit(solution)/shard_map/transport/pallas_call | solution.py:425
  33.9 2.3 %copy.6 = f32[8,16,16,128]{3,2,1,0:T(8,128)} copy(f32[8,16,16,128]{3,2,1,0:T(8,128)} %bitcast.3) | data formatting | bytes 2097152

commit v4 on v3

--- a/solution.py
+++ b/solution.py
@@ -28,17 +28,16 @@
     return a, b - e, c - f, d - g, -h
 
 
-def block_transpose(blocks, lane):
-    blocks = list(blocks)
-    for bit in (1, 2, 4):
-        odd = (lane // (16 * bit)) % 2 == 1
-        for g in range(8):
-            if g & bit:
-                continue
-            low, high = blocks[g], blocks[g + bit]
-            blocks[g] = jnp.where(odd, pltpu.roll(high, 16 * bit, 1), low)
-            blocks[g + bit] = jnp.where(odd, high, pltpu.roll(low, LANES - 16 * bit, 1))
-    return blocks
+def gathered(blocks, lane):
+    blocks = [pltpu.roll(block, 16 * g, 1) if g else block for g, block in enumerate(blocks)]
+    odd = [(lane // (16 * bit)) % 2 == 1 for bit in (1, 2, 4)]
+    full = []
+    for r in range(8):
+        parts = [blocks[(b - r) % 8] for b in range(8)]
+        for mask in odd:
+            parts = [jnp.where(mask, parts[n + 1], parts[n]) for n in range(0, len(parts), 2)]
+        full.append(pltpu.roll(parts[0], LANES - 16 * r, 1) if r else parts[0])
+    return full
 
 
 def kernel(
@@ -143,14 +142,17 @@
     def _():
         to_south.start()
 
-    halo_west = remote(
-        field0.at[pl.ds(2, 16), pl.ds(2, 2)], field0.at[pl.ds(2, 16), pl.ds(18, 2)],
-        halo_send.at[0], halo_recv.at[0], {"lon": west},
-    )
-    halo_east = remote(
-        field0.at[pl.ds(2, 16), pl.ds(16, 2)], field0.at[pl.ds(2, 16), pl.ds(0, 2)],
-        halo_send.at[1], halo_recv.at[1], {"lon": east},
-    )
+    def lon_copies(step, chunk):
+        field, rows = (field0, field1)[step], pl.ds(chunk * 4 + 2, 4)
+        to_w = remote(
+            field.at[rows, pl.ds(2, 2)], field.at[rows, pl.ds(18, 2)],
+            lon_send.at[step, 0, chunk], lon_recv.at[step, 0, chunk], {"lon": west},
+        )
+        to_e = remote(
+            field.at[rows, pl.ds(16, 2)], field.at[rows, pl.ds(0, 2)],
+            lon_send.at[step, 1, chunk], lon_recv.at[step, 1, chunk], {"lon": east},
+        )
+        return to_w, to_e
 
     def lat_copies(field, send, recv):
         to_s = remote(
@@ -163,9 +165,11 @@
         )
         return to_s, to_n
 
-    halo_south, halo_north = lat_copies(field0, halo_send.at[pl.ds(2, 2)], halo_recv.at[pl.ds(2, 2)])
-    halo_west.start()
-    halo_east.start()
+    halo_south, halo_north = lat_copies(field0, halo_send, halo_recv)
+    for copy in lon_copies(0, 2):
+        copy.start()
+    for copy in lon_copies(0, 1):
+        copy.start()
 
     @pl.when(has_south)
     def _():
@@ -174,6 +178,10 @@
     @pl.when(has_north)
     def _():
         halo_north.start()
+
+    for chunk in (0, 3):
+        for copy in lon_copies(0, chunk):
+            copy.start()
 
     send_gath(0)
 
@@ -213,13 +221,13 @@
         def unpack(c, _):
             for q in range(4):
                 rows = pl.ds(pl.multiple_of(c * 32 + q * 8, 8), 8)
-                full = block_transpose([gath[step, g, rows, :] for g in range(8)], lane)
+                full = gathered([gath[step, g, rows, :] for g in range(8)], lane)
                 for r in range(8):
                     courant[c, (q // 2) * 8 + r, 8 * (q % 2):8 * (q % 2) + 8, :] = full[r]
             return 0
 
         lax.fori_loop(0, 3, unpack, 0)
-        edges = block_transpose([ext[g] for g in range(8)], lane)
+        edges = gathered([ext[g] for g in range(8)], lane)
         for jb in range(2):
             courant[0, 16, 8 * jb:8 * jb + 8, :] = edges[2 * step + jb]
         for ib in range(2):
@@ -246,9 +254,11 @@
                         lat_faces(courant[1, i, pl.ds(8 * jb + 1, 8), :], row + 1),
                     )
                     up = jnp.where(lane == 0, 0.0, courant[2, i, here, :])
-                    low = faces(up, (lane == 1) | (lane == LANES - 1) | (lim[step, i, here, :] == 1))
-                    high = [pltpu.roll(x, LANES - 1, 1) for x in low]
-                    d2, d1, ver0, u1, u2 = spread(low, high)
+                    d2, b, c, d = faces(up, (lane == 1) | (lane == LANES - 1) | (lim[step, i, here, :] == 1))
+                    d1 = b - pltpu.roll(d2, LANES - 1, 1)
+                    ver0 = c - pltpu.roll(b, LANES - 1, 1)
+                    u1 = pltpu.roll(d, 2, 1) - pltpu.roll(c, 1, 1)
+                    u2 = -pltpu.roll(d, 1, 1)
                     every = (1.0 + lon0 + lat0 + ver0, w2, w1, e1, e2, s2, s1, n1, n2, d2, d1, u1, u2)
                     for point, value in enumerate(every):
                         coef[point, i, here, :] = value
@@ -268,9 +278,10 @@
                     c[5] * field[j, i + 2] + c[6] * field[j + 1, i + 2]
                     + c[7] * field[j + 3, i + 2] + c[8] * field[j + 4, i + 2]
                 )
+                below = pltpu.roll(q, 1, 1)
                 ver_part = (
-                    c[9] * pltpu.roll(q, 2, 1) + c[10] * pltpu.roll(q, 1, 1)
-                    + c[11] * pltpu.roll(q, LANES - 1, 1) + c[12] * pltpu.roll(q, LANES - 2, 1)
+                    c[9] * pltpu.roll(q, 2, 1) + c[10] * below
+                    + pltpu.roll(c[11] * below + c[12] * q, LANES - 2, 1)
                 )
                 new.append(c[0] * q + lon_part + (lat_part + ver_part))
             both = jnp.concatenate(new, axis=0)
@@ -284,20 +295,17 @@
         for i in range(16):
             write(j, i, total[8 * i:8 * i + 8])
 
-    def chunk_of(step, n):
-        if step == 0:
-            return (3 * n) % 4
-        late = n // 2
-        return late * (n - 2) + (1 - late) * (3 - n)
-
-    def row_of(step, n):
-        return chunk_of(step, n // 4) * 4 + n % 4
+    def chunk_of(n):
+        return 2 - n + 4 * (n // 3)
+
+    def row_of(n):
+        return chunk_of(n // 4) * 4 + n % 4
 
     def two_rows(step, field, n, write):
-        diffuse(step, row_of(step, jnp.maximum(n - 1, 0)), odd_split, write)
-        stencil(field, row_of(step, n), even_split)
-        diffuse(step, row_of(step, n), even_split, write)
-        stencil(field, row_of(step, n + 1), odd_split)
+        diffuse(step, row_of(jnp.maximum(n - 1, 0)), odd_split, write)
+        stencil(field, row_of(n), even_split)
+        diffuse(step, row_of(n), even_split, write)
+        stencil(field, row_of(n + 1), odd_split)
 
     for d, peer in enumerate(peers):
         remote(
@@ -311,51 +319,39 @@
         ).wait_recv()
     prepare(0)
 
-    halo_west.wait()
-    halo_east.wait()
-
-    @pl.when(has_south)
-    def _():
-        halo_south.wait_send()
-        halo_north.wait_recv()
-
-    @pl.when(has_north)
-    def _():
-        halo_north.wait_send()
-        halo_south.wait_recv()
-
-    def lon_copies(chunk):
-        rows = pl.ds(chunk * 4 + 2, 4)
-        to_w = remote(
-            field1.at[rows, pl.ds(2, 2)], field1.at[rows, pl.ds(18, 2)],
-            lon_send.at[0, chunk], lon_recv.at[0, chunk], {"lon": west},
-        )
-        to_e = remote(
-            field1.at[rows, pl.ds(16, 2)], field1.at[rows, pl.ds(0, 2)],
-            lon_send.at[1, chunk], lon_recv.at[1, chunk], {"lon": east},
-        )
-        return to_w, to_e
-
     next_south, next_north = lat_copies(field1, lat_send, lat_recv)
 
     def first_write(j, i, value):
         field1[j + 2, i + 2] = value
 
+    def take(step, n, to_s, to_n):
+        for copy in lon_copies(step, chunk_of(n)):
+            copy.wait()
+
+        @pl.when(jnp.logical_and(n == 2, has_south))
+        def _():
+            to_n.wait_recv()
+
+        @pl.when(jnp.logical_and(n == 3, has_north))
+        def _():
+            to_s.wait_recv()
+
     def give(n):
-        for copy in lon_copies(chunk_of(0, n)):
+        for copy in lon_copies(1, chunk_of(n)):
             copy.start()
 
-        @pl.when(jnp.logical_and(n == 0, has_south))
+        @pl.when(jnp.logical_and(n == 2, has_south))
         def _():
             next_south.start()
 
-        @pl.when(jnp.logical_and(n == 1, has_north))
+        @pl.when(jnp.logical_and(n == 3, has_north))
         def _():
             next_north.start()
 
     odd_split[...] = jnp.zeros((128, 256), jnp.bfloat16)
 
     def first_chunk(n, _):
+        take(0, n, halo_south, halo_north)
         two_rows(0, field0, 4 * n, first_write)
 
         @pl.when(n > 0)
@@ -366,7 +362,7 @@
         return 0
 
     lax.fori_loop(0, 4, first_chunk, 0)
-    diffuse(0, row_of(0, 15), odd_split, first_write)
+    diffuse(0, row_of(15), odd_split, first_write)
     give(3)
 
     for d, peer in enumerate(peers):
@@ -375,16 +371,6 @@
         ).wait()
     prepare(1)
 
-    @pl.when(has_south)
-    def _():
-        next_south.wait_send()
-        next_north.wait_recv()
-
-    @pl.when(has_north)
-    def _():
-        next_north.wait_send()
-        next_south.wait_recv()
-
     results = []
     for half in range(2):
         rows = pl.ds(8 * half, 8)
@@ -395,25 +381,31 @@
         done[pl.ds(i * 16 + j, 8, stride=256), :] = value
 
     def second_chunk(n, _):
-        for copy in lon_copies(chunk_of(1, n)):
-            copy.wait()
+        take(1, n, next_south, next_north)
         two_rows(1, field1, 4 * n, second_write)
 
-        @pl.when(n == 2)
-        def _():
-            results[1].start()
+        @pl.when(n == 3)
+        def _():
+            results[0].start()
 
         two_rows(1, field1, 4 * n + 2, second_write)
         return 0
 
     lax.fori_loop(0, 4, second_chunk, 0)
-    diffuse(1, row_of(1, 15), odd_split, second_write)
-    results[0].start()
+    diffuse(1, row_of(15), odd_split, second_write)
+    results[1].start()
     to_west.wait_send()
 
     @pl.when(has_south)
     def _():
         to_south.wait_send()
+        halo_south.wait_send()
+        next_south.wait_send()
+
+    @pl.when(has_north)
+    def _():
+        halo_north.wait_send()
+        next_north.wait_send()
 
     for result in results:
         result.wait()
@@ -447,8 +439,8 @@
             dma((2,)), dma((2,)),
             dma((7,)), dma((7,)),
             dma((2, 7)), dma((2, 7)),
-            dma((4,)), dma((4,)),
-            dma((2, 4)), dma((2, 4)),
+            dma((2,)), dma((2,)),
+            dma((2, 2, 4)), dma((2, 2, 4)),
             dma((2,)), dma((2,)),
         ],
         compiler_params=pltpu.CompilerParams(

time: 36.3 us -> 36.1 us (level)
  Pallas kernels: 33.8 us -> 33.4 us
    pallas_call x1, Pallas kernels: 33.8 us -> 33.4 us  [on_device(): pl.pallas_call(kernel, out_shape=jax.ShapeDtypeStruct((128, 16, LANES), f...]
where the time goes in v4:
time: 36.1 us; the launch traced here: 35.7 us
  Pallas kernels  33.4 us (93%)
  local copies, waits for them, and re-layouts  2.27 us (6%)
    pallas_call x1, Pallas kernels, on_device(): pl.pallas_call(kernel, out_shape=jax.ShapeDtypeStruct((128, 16, LANES), f...  33.4 us
    unnamed x1, local copies, waits for them, and re-layouts  2.27 us

profile of v4, /device:TPU:1, one launch (start us, length us, event | category | flops | bytes accessed | tf_op | source)
XLA Modules:
  0.0 35.7 jit_solution(16401683440633459430)
XLA Ops:
  0.0 33.4 %transport.1 = f32[128,16,128]{2,1,0:T(8,128)} custom-call(f32[2048,128]{1,0:T(8,128)} %bitcast.4, f32[2,768,16]{2,1,0:T(8,128)} %bitcast.5, s32[2,16,16,128]{3,2,1,0:T(8,128)} %limiter.1, f32[2,16,128,128]{3,2,1,0:T(8,128)} %inverse.1), custom_call_target="tpu_custom_call" | custom-call | tf_op jit(solution)/shard_map/transport/pallas_call | solution.py:417
  33.4 2.3 %copy.6 = f32[8,16,16,128]{3,2,1,0:T(8,128)} copy(f32[8,16,16,128]{3,2,1,0:T(8,128)} %bitcast.3) | data formatting | bytes 2097152
